TPU v7x, 512 devices: a whole 4x4x16 slice. The times are simulated.
512 devices in a mesh: dp: 64 (over y_lo, z, core), fsdp: 8 (over x, y_hi).
Axes of the slice: x: 4, y: 4 (y_hi: 2, y_lo: 2; y = y_hi * 2 + y_lo), z: 16, core: 2. Of those that a mesh axis runs over, the one named last changes fastest.
Arguments:
- tokens: bfloat16 [262144, 1024], P(('dp', 'fsdp')), may hold values from -6 to 6
- w_in: bfloat16 [1024, 2048], P('fsdp'), may hold values from -0.1875 to 0.1875
- b_in: float32 [2048], replicated, may hold values from -3 to 3
- w_out: bfloat16 [2048, 1024], P('fsdp'), may hold values from -0.125 to 0.125
- b_out: float32 [1024], replicated, may hold values from -2 to 2
- ln_gain: float32 [1024], replicated, may hold values from 0.5 to 1.5
- ln_bias: float32 [1024], replicated, may hold values from -1.5 to 1.5
- head: bfloat16 [1024, 1024], replicated, may hold values from -0.1875 to 0.1875
- query_feats: bfloat16 [2048, 1024], P(('dp', 'fsdp')), may hold values from -6 to 6
- positive_rows: bfloat16 [2048, 1024], P(('dp', 'fsdp')), may hold values from -1 to 1
- neg_ids: int32 [2048, 64], P(('dp', 'fsdp')), may hold values from 0 to 2047, as said below
Outputs:
- refreshed: bfloat16 [2048, 1024], P(('dp', 'fsdp'))
- loss: float32 [2048], P(('dp', 'fsdp'))
- head_grad: float32 [1024, 1024], P('fsdp')
Inputs may be any that keep to these rules, and one draw needn't show every extreme that they name: `neg_ids`: in each aligned block of 4 queries (the queries of one device), ids in one range [g * 32, (g + 1) * 32) appear at most 16 times among the block's entries, and some range exactly 16 times.
All inputs are finite; a program needn't handle non-finite values.
Results may differ from a plain program's by a relative error of at most 0.012.
The roundings to bfloat16 on the way count: a program that leaves them out, or rounds other values in their place, can miss the bound.
Values may be sent and summed in bfloat16 or wider, within the bound.
A program may use at most 64 MiB of HBM per device.

v0:
```python
import jax
import jax.numpy as jnp
from jax import lax
from jax.sharding import PartitionSpec as P

SEQ = 128


score_scale = 0.5
eps = 1e-05


def body(
    tokens, w_in, b_in, w_out, b_out, ln_gain, ln_bias, head, query_feats, positive_rows, neg_ids
):
    width = tokens.shape[1]
    columns = tokens
    pre = jnp.dot(
        columns,
        lax.all_gather(w_in, "fsdp", axis=0, tiled=True),
        preferred_element_type=jnp.float32,
    )
    hidden = jax.nn.gelu(pre + b_in, approximate=True).astype(jnp.bfloat16)
    columns = hidden
    ffn = jnp.dot(
        columns,
        lax.all_gather(w_out, "fsdp", axis=0, tiled=True),
        preferred_element_type=jnp.float32,
    )
    summed = tokens.astype(jnp.float32) + ffn + b_out
    center = summed - jnp.mean(summed, axis=-1, keepdims=True)
    spread = jnp.mean(center * center, axis=-1, keepdims=True)
    normed = center * lax.rsqrt(spread + eps) * ln_gain + ln_bias
    embedded = jnp.mean(normed.reshape(-1, SEQ, width), axis=1).astype(jnp.bfloat16)
    group = lax.all_gather(embedded, "fsdp", axis=0, tiled=True)
    query = jnp.dot(query_feats, head, preferred_element_type=jnp.float32).astype(jnp.bfloat16)
    ids_flat = neg_ids.reshape(-1)
    piece = lax.all_gather(group, "dp", axis=0, tiled=True)
    match = ids_flat[:, None] == jnp.arange(piece.shape[0], dtype=jnp.int32)[None, :]
    picked = jnp.dot(match.astype(jnp.bfloat16), piece, preferred_element_type=jnp.float32)
    neg_rows = picked.astype(jnp.bfloat16)
    neg_rows = neg_rows.reshape(neg_ids.shape[0], neg_ids.shape[1], width)
    s_neg = score_scale * jnp.einsum(
        "qd,qkd->qk", query, neg_rows, preferred_element_type=jnp.float32
    )
    s_pos = score_scale * jnp.sum(
        query.astype(jnp.float32) * positive_rows.astype(jnp.float32), axis=-1
    )
    top = jnp.maximum(s_pos, jnp.max(s_neg, axis=-1))
    total = top + jnp.log(jnp.exp(s_pos - top) + jnp.sum(jnp.exp(s_neg - top[:, None]), axis=-1))
    loss = total - s_pos
    weights = jnp.exp(s_neg - total[:, None]).astype(jnp.bfloat16)
    mixed = jnp.einsum("qk,qkd->qd", weights, neg_rows, preferred_element_type=jnp.float32)
    coeff = jnp.exp(s_pos - total) - 1.0
    dquery = (score_scale * (coeff[:, None] * positive_rows.astype(jnp.float32) + mixed)).astype(
        jnp.bfloat16
    )
    share = width // lax.axis_size("fsdp")
    offset = lax.axis_index("fsdp") * share
    term = jnp.einsum("qa,qb->ab", query_feats, dquery, preferred_element_type=jnp.float32)
    summed_grad = lax.psum(term, ("dp", "fsdp"))
    head_grad = lax.dynamic_slice_in_dim(summed_grad, offset, share, 0)
    return (embedded, loss, head_grad)


def solution(mesh):
    in_specs = (
        P(("dp", "fsdp"), None),
        P("fsdp", None),
        P(),
        P("fsdp", None),
        P(),
        P(),
        P(),
        P(),
        P(("dp", "fsdp"), None),
        P(("dp", "fsdp"), None),
        P(("dp", "fsdp"), None),
    )
    out_specs = (P(("dp", "fsdp"), None), P(("dp", "fsdp")), P("fsdp", None))
    return jax.shard_map(body, mesh=mesh, in_specs=in_specs, out_specs=out_specs, check_vma=False)
```

profile of v0, /device:TPU:1, one launch (start us, length us, event | category | flops | bytes accessed | tf_op | source)
XLA Modules:
  0.0 862.9 jit_solution(12246609236654953071)
XLA Ops:
  7.2 0.7 all-gather.5.cloned.1.call-update
  8.0 0.7 all-gather.7.cloned.1.call-update
  8.7 94.4 %all-gather.5.cloned.1.call-done = bf16[1024,2048]{1,0:T(8,128)(2,1)} async-done(((bf16[128,2048]{1,0:T(8,128)(2,1)}), bf16[1024,2048]{1,0:T(8,128)(2,1)}) %all-gather.5.cloned.1.call-update) | async-done | bytes 4194320 | tf_op jit(solution)/shard_map/all_gather | solution.py:20
  103.1 88.2 %all-gather.7.cloned.1.call-done = bf16[2048,1024]{1,0:T(8,128)(2,1)} async-done(((bf16[256,1024]{1,0:T(8,128)(2,1)}), bf16[2048,1024]{1,0:T(8,128)(2,1)}) %all-gather.7.cloned.1.call-update) | async-done | bytes 4194320 | tf_op jit(solution)/shard_map/all_gather | solution.py:27
  191.3 10.2 %fusion.30 = (f32[512]{0:T(512)S(1)}, f32[512,1024]{1,0:T(8,128)}) fusion(f32[1024]{0:T(1024)} %param.15, bf16[2048,1024]{1,0:T(8,128)(2,1)} %all-gather.7.cloned.1.call-done, bf16[512,1024]{1,0:T(8,128)(2,1)} %param.11, bf16[1024,2048]{1,0:T(8,128)(2,1)} %all-gather.5.cloned.1.call-done, f32[2048]{0:T(1024)} %param.13), kind=kOutput, calls=%fused_computation.49 | convolution fusion | flops 4307549696 | bytes 11548672 | tf_op jit(solution)/shard_map/dot_general | solution.py:25
  201.5 2.0 multiply_reduce_fusion
  203.5 2.1 bitcast_reduce_fusion
  205.6 27.8 %all-gather = bf16[8,4,1024]{2,1,0:T(4,128)(2,1)S(1)} all-gather(bf16[1,4,1024]{2,1,0:T(4,128)(2,1)S(1)} %fusion.40), channel_id=1, replica_groups=mesh['dp'=64,'fsdp'=8] {'fsdp'}, dimensions={0}, use_global_device_ids=true | all-gather | bytes 73728 | tf_op jit(solution)/shard_map/all_gather | solution.py:35
  233.4 0.6 reshape.58
  234.1 0.1 eq.15
  234.2 0.5 fusion.11
  234.7 128.5 %all-gather.9.cloned.1.call-done = bf16[2048,1024]{1,0:T(8,128)(2,1)} async-done(((bf16[32,1024]{1,0:T(8,128)(2,1)}), bf16[2048,1024]{1,0:T(8,128)(2,1)}) %all-gather.9.cloned.1.call-update) | async-done | bytes 4194320 | tf_op jit(solution)/shard_map/all_gather | solution.py:38
  363.2 3.5 fusion.9
  366.7 0.2 fusion.15
  366.9 0.1 multiply_reduce_fusion.1
  367.0 0.2 exponential_reduce_fusion
  367.3 0.1 fusion.22
  367.3 0.2 fusion.20
  367.5 2.8 convolution_bitcast_fusion
  370.3 0.6 multiply_convert_fusion
  371.0 0.5 fusion.28
  371.5 482.8 %all-reduce.2.cloned.1.call-done = f32[1024,1024]{0,1:T(8,128)} async-done(((f32[1024,1024]{0,1:T(8,128)}), f32[1024,1024]{0,1:T(8,128)}) %all-reduce.2.cloned.1.call-update) | async-done | bytes 4194320 | tf_op jit(solution)/shard_map/psum | solution.py:61
  854.3 1.1 constant_dynamic-slice_fusion
  855.4 1.0 copy.16
  (23 shorter events, 0.3 us)
Async XLA Ops:
  7.2 227.0 %copy-start = (bf16[1024,1024]{1,0:T(8,128)(2,1)S(1)}, bf16[1024,1024]{1,0:T(8,128)(2,1)}, u32[]{:S(2)}) copy-start(bf16[1024,1024]{1,0:T(8,128)(2,1)} %param.18) | copy-start | bytes 6291460
  7.2 95.9 %all-gather.5.cloned.1.call-start = ((), (), s32[]{:S(2)}) async-start(), calls=%async_computation | async-start | bytes 4718592 | tf_op jit(solution)/shard_map/all_gather | solution.py:20
  7.9 183.4 %all-gather.7.cloned.1.call-start = ((), (), s32[]{:S(2)}) async-start(), calls=%async_computation.1 | async-start | bytes 4718592 | tf_op jit(solution)/shard_map/all_gather | solution.py:27
  8.7 194.8 %copy-start.3 = (f32[1024]{0:T(1024)S(1)}, f32[1024]{0:T(1024)}, u32[]{:S(2)}) copy-start(f32[1024]{0:T(1024)} %param.17) | copy-start | bytes 12292
  8.7 194.8 %copy-start.4 = (f32[1024]{0:T(1024)S(1)}, f32[1024]{0:T(1024)}, u32[]{:S(2)}) copy-start(f32[1024]{0:T(1024)} %param.16) | copy-start | bytes 12292
  8.7 354.5 %all-gather.9.cloned.1.call-start = ((), (), s32[]{:S(2)}) async-start(), calls=%async_computation.2 | async-start | bytes 4259840 | tf_op jit(solution)/shard_map/all_gather | solution.py:38
  201.5 32.6 %copy-start.5 = (s32[4,64]{1,0:T(4,128)S(1)}, s32[4,64]{1,0:T(4,128)}, u32[]{:S(2)}) copy-start(s32[4,64]{1,0:T(4,128)} %param.21) | copy-start | bytes 3076
  201.5 32.7 %copy-start.1 = (bf16[4,1024]{1,0:T(4,128)(2,1)S(1)}, bf16[4,1024]{1,0:T(4,128)(2,1)}, u32[]{:S(2)}) copy-start(bf16[4,1024]{1,0:T(4,128)(2,1)} %param.20) | copy-start | bytes 24580
  201.5 32.7 %copy-start.2 = (bf16[4,1024]{1,0:T(4,128)(2,1)S(1)}, bf16[4,1024]{1,0:T(4,128)(2,1)}, u32[]{:S(2)}) copy-start(bf16[4,1024]{1,0:T(4,128)(2,1)} %param.19) | copy-start | bytes 24580
  234.0 620.3 %all-reduce.2.cloned.1.call-start = ((), (), s32[]{:S(2)}) async-start(), calls=%async_computation.3 | async-start | bytes 8388608 | tf_op jit(solution)/shard_map/psum | solution.py:61
Sparse Core Ops, SparseCore 0:
  11.2 91.8 all-gather.4
  106.3 84.9 all-gather.6
  234.2 128.9 all-gather.8
  370.5 483.7 all-reduce.1
where the time goes:
time: 865 us; the launch traced here: 863 us
  waiting for transfers between devices  795 us (92%)
  blocking collectives  27.8 us (3%)
  matrix products  17.3 us (2%)
  between operations  13.9 us (2%)
    psum x1, waiting for transfers between devices, body(): summed_grad = lax.psum(term, ('dp', 'fsdp'))  483 us
    all_gather x1, waiting for transfers between devices, body(): piece = lax.all_gather(group, 'dp', axis=0, tiled=True)  128 us
    all_gather x1, waiting for transfers between devices, body(): lax.all_gather(w_in, 'fsdp', axis=0, tiled=True)  94.4 us
    all_gather x1, waiting for transfers between devices, body(): lax.all_gather(w_out, 'fsdp', axis=0, tiled=True)  88.2 us
    all_gather x1, blocking collectives, body(): group = lax.all_gather(embedded, 'fsdp', axis=0, tiled=True)  27.8 us
  transfers between devices with their start and end apart: 4, of which 4 were waited for; matrix products, arithmetic and copies ran while one was open for 0% of the time, Pallas kernels for 0%

commit v1 on v0

v1 whole, which is shorter than its diff:
```python
import jax
import jax.numpy as jnp
from jax import lax
from jax.experimental import pallas as pl
from jax.experimental.pallas import tpu as pltpu
from jax.sharding import PartitionSpec as P

SEQ = 128
NX, NZ, NF, NPLANE = 4, 16, 8, 32
score_scale = 0.5
eps = 1e-05
LOW = -3.0e38
MESH = pl.DeviceIdType.MESH
F32, BF16 = jnp.float32, jnp.bfloat16


def iota(shape, dim):
    return lax.broadcasted_iota(jnp.int32, shape, dim)


def dot(a, b, dims=(1, 0)):
    return lax.dot_general(
        a, b, (((dims[0],), (dims[1],)), ((), ())), preferred_element_type=F32
    )


def pick(mask):
    return mask.astype(F32).astype(BF16)


def take_all(ref, sem):
    pltpu.make_async_copy(ref, ref, sem).wait()


def kernel(
    tok, win, b_in, wout, b_out, gain, bias, head, feats, pos, ids,
    emb, loss, hg,
    W1, W2, hid, summed, stg, qf16, idsb, pos16, r16, qfs, qfr, query, queryf, posf, idst, cT, rk,
    stb, wr, gr, rss, rsr, agr,
    xl, xr, fl, fr, orv, srv, sa, sb, ssend, loc,
    zq, zi, pp, fq, rp, zs, fw, gx, zr, za, ga, psend,
):
    dp, f = lax.axis_index("dp"), lax.axis_index("fsdp")
    yl, z, c = dp // 32, (dp // 2) % NZ, dp % 2
    x, yh = f // 2, f % 2
    k = yl * 2 + c
    d = k * NF + f

    def chip(xx, hh, ll, cc):
        return (ll * 32 + z * 2 + cc, xx * 2 + hh)

    right, left = chip((x + 1) % NX, yh, yl, c), chip((x + 3) % NX, yh, yl, c)
    other, same = chip(x, 1 - yh, 1 - yl, c), chip(x, yh, 1 - yl, c)
    sibling = chip(x, yh, yl, 1 - c)

    def plane_peer(i):
        e = (d + i) % NPLANE
        return ((e // 16) * 32 + z * 2 + (e // 8) % 2, e % NF)

    def z_at(n):
        away = NZ // 2 + ((n + 1) // 2) * (2 * (n % 2) - 1)
        return (z + away) % NZ

    def z_peer(zz):
        return (yl * 32 + zz * 2 + c, f)

    def f_at(i):
        return (f + i) % NF

    def quarter_peer(i):
        e = (k + i) % 4
        return ((e // 2) * 32 + z * 2 + e % 2, f)

    def send(src, dst, ss, rs, to):
        copy = pltpu.make_async_remote_copy(
            src_ref=src, dst_ref=dst, send_sem=ss, recv_sem=rs, device_id=to, device_id_type=MESH
        )
        copy.start()
        return copy

    barrier = pltpu.get_barrier_semaphore()

    @pl.loop(1, NPLANE)
    def _(i):
        pl.semaphore_signal(barrier, inc=1, device_id=plane_peer(i), device_id_type=MESH)

    @pl.loop(0, NZ - 1)
    def _(n):
        pl.semaphore_signal(barrier, inc=1, device_id=z_peer(z_at(n)), device_id_type=MESH)

    def spread(rows):
        for i in range(4):
            for j in range(4):
                stg[pl.ds(i * 4 + j, 1), :] = rows[i : i + 1, j * 256 : (j + 1) * 256]
        return stg[...].astype(BF16)

    qf16[z] = spread(feats[...].astype(F32))
    pos16[d] = spread(pos[...].astype(F32))
    posf[...] = jnp.zeros_like(posf)
    posf[0:4, :] = pos[...].astype(F32)
    idsb[z] = jnp.full((8, 128), -1, jnp.int32)
    idsb[z, 0:4, 0:64] = ids[...]

    pl.semaphore_wait(barrier, NPLANE - 1 + NZ - 1)

    def stage(s):
        if s < 2:
            return win, W1, pl.ds(s * 1024, 1024)
        return wout, W2, pl.ds((s - 2) * 512, 512)

    sent = []

    def out(s, n, src, dst, rs, to):
        sent.append(send(src, dst, ssend.at[s, n], rs, to))

    def landed(ref, sem):
        take_all(ref, sem)

    def own(s):
        shard, W, cols = stage(s)
        src = shard.at[c, :, :, cols]
        dst = W.at[x, yh, c, :, :, cols]
        out(s, 0, src, dst, xl.at[s], right)
        out(s, 1, src, dst, xr.at[s], left)
        out(s, 2, shard.at[c, 1 - yl, :, cols], W.at[x, yh, c, 1 - yl, :, cols], orv.at[s], other)

    xm, xp, xo = (x + 3) % NX, (x + 1) % NX, (x + 2) % NX

    def first(s):
        _, W, cols = stage(s)
        landed(W.at[xm, yh, c, :, :, cols], xl.at[s])
        out(s, 3, W.at[xm, yh, c, 0, :, cols], W.at[xm, yh, c, 0, :, cols], fl.at[s], right)
        half = W.at[xm, yh, c, 1 - yl, :, cols]
        out(s, 4, half, half, orv.at[s], other)
        landed(W.at[xp, yh, c, :, :, cols], xr.at[s])
        out(s, 5, W.at[xp, yh, c, 1, :, cols], W.at[xp, yh, c, 1, :, cols], fr.at[s], left)
        half = W.at[xp, yh, c, 1 - yl, :, cols]
        out(s, 6, half, half, orv.at[s], other)

    def second(s):
        _, W, cols = stage(s)
        landed(W.at[xo, yh, c, 0, :, cols], fl.at[s])
        landed(W.at[xo, yh, c, 1, :, cols], fr.at[s])
        half = W.at[xo, yh, c, 1 - yl, :, cols]
        out(s, 7, half, half, orv.at[s], other)
        mine = W.at[:, yh, c, :, :, cols]
        out(s, 8, mine, mine, sa.at[s], sibling)

    def third(s):
        _, W, cols = stage(s)
        theirs = W.at[:, 1 - yh, c, yl, :, cols]
        landed(theirs, orv.at[s])
        out(s, 9, theirs, theirs, srv.at[s], same)

    def fourth(s):
        _, W, cols = stage(s)
        landed(W.at[:, 1 - yh, c, 1 - yl, :, cols], srv.at[s])
        theirs = W.at[:, 1 - yh, c, :, :, cols]
        out(s, 10, theirs, theirs, sb.at[s], sibling)

    def whole(s):
        _, W, cols = stage(s)
        landed(W.at[:, yh, 1 - c, :, :, cols], sa.at[s])
        landed(W.at[:, 1 - yh, 1 - c, :, :, cols], sb.at[s])

    def compute(s):
        if s < 2:

            @pl.loop(0, 4)
            def _(n):
                at = pl.ds(pl.multiple_of(s * 1024 + n * 256, 256), 256)
                w = W1[:, :, :, :, :, at].reshape(1024, 256)
                v = dot(tok[...], w) + b_in[:, at]
                g = 0.5 * v * (1.0 + jnp.tanh(0.7978845608 * (v + 0.044715 * (v * v * v))))
                hid[:, at] = g.astype(BF16)
        else:

            @pl.loop(0, 2)
            def _(n):
                at = pl.ds(pl.multiple_of((s - 2) * 512 + n * 256, 256), 256)
                w = W2[:, :, :, :, :, at].reshape(2048, 256)
                summed[:, at] = tok[:, at].astype(F32) + dot(hid[...], w) + b_out[:, at]

    own(0)
    own(1)
    keep1 = pltpu.make_async_copy(win.at[c], W1.at[x, yh, c], loc.at[0])
    keep2 = pltpu.make_async_copy(wout.at[c], W2.at[x, yh, c], loc.at[1])
    keep1.start()
    keep2.start()

    @pl.loop(0, NZ - 1)
    def _(n):
        to = z_peer(z_at(n))
        send(qf16.at[z], qf16.at[z], psend.at[0], zq.at[0], to)
        send(idsb.at[z], idsb.at[z], psend.at[1], zi.at[0], to)

    keep1.wait()
    keep2.wait()

    first(0)
    own(2)
    second(0)
    first(1)
    own(3)

    take_all(qf16.at[pl.ds(0, NZ - 1)], zq.at[0])
    flat = qf16[...].reshape(NZ * 16, 256)
    for j in range(4):
        sel = pick(iota((64, 256), 1) == 4 * iota((64, 256), 0) + j)
        rows = dot(sel, flat).astype(BF16)
        qfs[2 * j] = rows[:, :128]
        qfs[2 * j + 1] = rows[:, 128:]
    qfr[f] = qfs[f]

    @pl.loop(1, NF)
    def _(i):
        to = f_at(i)
        send(qfs.at[to], qfr.at[f], psend.at[2], fq.at[0], (dp, to))

    third(0)
    second(1)
    first(2)

    @pl.loop(1, NPLANE)
    def _(i):
        send(pos16.at[d], pos16.at[d], psend.at[3], pp.at[0], plane_peer(i))

    fourth(0)
    third(1)
    second(2)

    total_q = jnp.zeros((128, 1024), F32)
    m = iota((128, 256), 0)
    for j in range(4):
        sel = pick((iota((128, 256), 1) == (m // 8) * 16 + (m % 8) * 4 + j) & (m % 8 < 4))
        rows = dot(sel, flat).astype(BF16)
        total_q = total_q + dot(rows, head[j * 256 : (j + 1) * 256, :])
    query[...] = total_q.astype(BF16)
    queryf[...] = query[...].astype(F32)

    first(3)
    whole(0)
    compute(0)
    fourth(1)
    third(2)
    second(3)

    take_all(idsb.at[pl.ds(0, NZ - 1)], zi.at[0])
    idst[...] = jnp.transpose(idsb[...].reshape(128, 128).astype(F32))
    pi = iota((128, 1), 0)
    pid = (((pi // 64) * 32 + z * 2 + (pi // 32) % 2) * NF + (pi // 4) % NF) * 4 + pi % 4
    pid = pid.astype(F32)
    cT[...] = lax.fori_loop(
        0, 64,
        lambda t, a: a + (idst[pl.ds(t, 1), :] == pid).astype(F32),
        jnp.zeros((128, 128), F32),
    )

    third(3)
    whole(1)
    compute(1)
    fourth(2)
    fourth(3)
    whole(2)
    compute(2)
    whole(3)
    compute(3)

    rows = []
    for i in range(4):
        v = summed[i * SEQ : (i + 1) * SEQ, :]
        center = v - jnp.mean(v, axis=-1, keepdims=True)
        spread_ = jnp.mean(center * center, axis=-1, keepdims=True)
        normed = center * lax.rsqrt(spread_ + eps)
        rows.append(jnp.sum(normed, axis=0, keepdims=True) * (1.0 / SEQ) * gain[...] + bias[...])
    pooled = jnp.concatenate(rows, axis=0)
    emb[...] = pooled.astype(BF16)
    r16[d] = spread(pooled)

    @pl.loop(1, NPLANE)
    def _(i):
        send(r16.at[d], r16.at[d], psend.at[4], rp.at[0], plane_peer(i))

    lane = iota((1, 128), 1)
    mine = (lane // 8 == z) & (lane % 8 < 4)
    s_col = score_scale * jnp.sum(
        queryf[pl.ds(pl.multiple_of(z * 8, 8), 8), :] * posf[...], axis=-1, keepdims=True
    )
    s_pos = jnp.sum(
        jnp.where(iota((8, 128), 1) == z * 8 + iota((8, 128), 0), s_col, 0.0), axis=0, keepdims=True
    )

    take_all(r16.at[pl.ds(0, NPLANE - 1)], rp.at[0])
    flat_r = r16[...].reshape(NPLANE * 16, 256)
    s = jnp.zeros((128, 128), F32)
    for j in range(4):
        sel = pick(iota((128, 512), 1) == 4 * iota((128, 512), 0) + j)
        rows = dot(sel, flat_r).astype(BF16)
        rk[j] = rows
        s = s + dot(rows, query[:, j * 256 : (j + 1) * 256], (1, 1))
    s = s * score_scale
    count = cT[...]
    listed = count > 0.0
    high = jnp.max(jnp.where(listed, s, LOW), axis=0, keepdims=True)
    part = jnp.sum(
        jnp.where(listed, count * jnp.exp(jnp.where(listed, s - high, 0.0)), 0.0), axis=0, keepdims=True
    )
    high2 = jnp.where(mine, jnp.maximum(high, s_pos), high)
    part2 = part * jnp.exp(high - high2) + jnp.where(mine, jnp.exp(s_pos - high2), 0.0)
    r8 = iota((8, 128), 0)
    stb[z] = jnp.where(r8 == 0, high2, jnp.where(r8 == 1, part2, 0.0))

    @pl.loop(0, NZ - 1)
    def _(n):
        send(stb.at[z], stb.at[z], psend.at[5], zs.at[0], z_peer(z_at(n)))

    take_all(stb.at[pl.ds(0, NZ - 1)], zs.at[0])
    stats = stb[...]
    highs, parts = stats[:, 0, :], stats[:, 1, :]
    top = jnp.max(highs, axis=0, keepdims=True)
    total = top + jnp.log(jnp.sum(parts * jnp.exp(highs - top), axis=0, keepdims=True))
    loss[...] = jnp.where(r8 == 0, jnp.where(mine, total - s_pos, 0.0), 0.0)
    coeff = jnp.where(mine, jnp.exp(jnp.where(mine, s_pos - total, 0.0)) - 1.0, 0.0)
    w = jnp.exp(jnp.where(listed, s - total, 0.0)).astype(BF16).astype(F32)
    w = jnp.where(listed, count * w, 0.0).astype(BF16)
    j64 = iota((64, 128), 0)
    wr[f, 0:64, :] = dot(pick(iota((64, 128), 1) == (j64 // 4) * 8 + j64 % 4), w, (1, 1)).astype(BF16)
    c0 = coeff.astype(BF16).astype(F32)
    c1 = (coeff - c0).astype(BF16).astype(F32)
    c2 = coeff - c0 - c1
    r16i = iota((16, 128), 0)
    wr[f, 64:80, :] = jnp.where(
        r16i == 0, c0, jnp.where(r16i == 1, c1, jnp.where(r16i == 2, c2, 0.0))
    ).astype(BF16)

    @pl.loop(1, NF)
    def _(i):
        send(wr.at[f], wr.at[f], psend.at[6], fw.at[0], (dp, f_at(i)))

    take_all(pos16.at[pl.ds(0, NPLANE - 1)], pp.at[0])
    sel = pick(iota((128, 512), 1) == 4 * iota((128, 512), 0) + k)
    pos_k = dot(sel, pos16[...].reshape(NPLANE * 16, 256)).astype(BF16)
    take_all(qfr.at[pl.ds(0, NF - 1)], fq.at[0])
    slices = qfr[...].reshape(NF * 64, 128)
    g32 = iota((32, 512), 0)
    group_q = dot(pick(iota((32, 512), 1) == (g32 // 4) * 64 + z * 4 + g32 % 4), slices)

    take_all(wr.at[pl.ds(0, NF - 1)], fw.at[0])
    g_part = dot(wr[:, 0:64, :].reshape(NF * 64, 128), slices, (0, 0))
    e32, l32 = iota((32, 128), 0), iota((32, 128), 1)
    expand = pick((l32 // 16 == e32 // 4) & (l32 % 16 < 3))
    co = dot(expand, wr[:, 64:80, :].reshape(128, 128))
    co = jnp.sum(jnp.where(l32 == z * 8 + e32 % 4, co, 0.0), axis=1, keepdims=True)
    gr[k, 0:128, :] = g_part.astype(BF16)
    gr[k, 128:160, :] = (group_q * co).astype(BF16)

    @pl.loop(1, 4)
    def _(i):
        send(gr.at[k], gr.at[k], psend.at[7], gx.at[0], quarter_peer(i))

    take_all(gr.at[pl.ds(0, 3)], gx.at[0])
    g_all = gr[...]
    g_sum = jnp.sum(g_all[:, 0:128, :].astype(F32), axis=0).astype(BF16)
    g_pos = g_all[:, 128:160, :].reshape(128, 128)
    term = score_scale * (dot(g_sum, rk[k], (0, 0)) + dot(g_pos, pos_k, (0, 0)))
    for t in range(NZ):
        rss[t] = term[(t // 2) * 16 : (t // 2) * 16 + 16, (t % 2) * 128 : (t % 2) * 128 + 128]
    rsr[z] = rss[z]

    @pl.loop(0, NZ - 1)
    def _(n):
        to = z_at(n)
        send(rss.at[to], rsr.at[z], psend.at[8], zr.at[0], z_peer(to))

    take_all(rsr.at[pl.ds(0, NZ - 1)], zr.at[0])
    agr[k, z] = jnp.sum(rsr[...], axis=0).astype(BF16)

    @pl.loop(0, NZ - 1)
    def _(n):
        send(agr.at[k, z], agr.at[k, z], psend.at[9], za.at[0], z_peer(z_at(n)))

    take_all(agr.at[k, pl.ds(0, NZ - 1)], za.at[0])

    @pl.loop(1, 4)
    def _(i):
        send(agr.at[k], agr.at[k], psend.at[10], ga.at[0], quarter_peer(i))

    take_all(agr.at[pl.ds(0, 3)], ga.at[0])
    for e in range(4):
        for t in range(NZ):
            at = e * 256 + (t % 2) * 128
            hg[(t // 2) * 16 : (t // 2) * 16 + 16, at : at + 128] = agr[e, t].astype(F32)

    for copy in sent:
        copy.wait_send()
    take_all(qf16.at[pl.ds(0, NZ - 1)], psend.at[0])
    take_all(idsb.at[pl.ds(0, NZ - 1)], psend.at[1])
    take_all(qfr.at[pl.ds(0, NF - 1)], psend.at[2])
    take_all(pos16.at[pl.ds(0, NPLANE - 1)], psend.at[3])
    take_all(r16.at[pl.ds(0, NPLANE - 1)], psend.at[4])
    take_all(stb.at[pl.ds(0, NZ - 1)], psend.at[5])
    take_all(wr.at[pl.ds(0, NF - 1)], psend.at[6])
    take_all(gr.at[pl.ds(0, 3)], psend.at[7])
    take_all(rsr.at[pl.ds(0, NZ - 1)], psend.at[8])
    take_all(agr.at[0, pl.ds(0, NZ - 1)], psend.at[9])
    take_all(agr.at[pl.ds(0, 3)], psend.at[10])


def body(
    tokens, w_in, b_in, w_out, b_out, ln_gain, ln_bias, head, query_feats, positive_rows, neg_ids
):
    vmem = pl.BlockSpec(memory_space=pltpu.VMEM)
    V, S = pltpu.VMEM, pltpu.SemaphoreType.DMA
    embedded, loss, head_grad = pl.pallas_call(
        kernel,
        out_shape=(
            jax.ShapeDtypeStruct((4, 1024), BF16),
            jax.ShapeDtypeStruct((8, 128), F32),
            jax.ShapeDtypeStruct((128, 1024), F32),
        ),
        in_specs=[vmem] * 11,
        out_specs=(vmem,) * 3,
        scratch_shapes=[
            V((4, 2, 2, 2, 32, 2048), BF16),
            V((4, 2, 2, 2, 64, 1024), BF16),
            V((512, 2048), BF16),
            V((512, 1024), F32),
            V((16, 256), F32),
            V((NZ, 16, 256), BF16),
            V((NZ, 8, 128), jnp.int32),
            V((NPLANE, 16, 256), BF16),
            V((NPLANE, 16, 256), BF16),
            V((NF, 64, 128), BF16),
            V((NF, 64, 128), BF16),
            V((128, 1024), BF16),
            V((128, 1024), F32),
            V((8, 1024), F32),
            V((128, 128), F32),
            V((128, 128), F32),
            V((4, 128, 256), BF16),
            V((NZ, 8, 128), F32),
            V((NF, 80, 128), BF16),
            V((4, 160, 128), BF16),
            V((NZ, 16, 128), F32),
            V((NZ, 16, 128), F32),
            V((4, NZ, 16, 128), BF16),
        ]
        + [S((4,))] * 8
        + [S((4, 11)), S((2,))]
        + [S((1,))] * 11
        + [S((11,))],
        compiler_params=pltpu.CompilerParams(
            collective_id=0, has_side_effects=True, vmem_limit_bytes=48 << 20
        ),
    )(
        tokens,
        w_in.reshape(2, 2, 32, 2048),
        b_in.reshape(1, -1),
        w_out.reshape(2, 2, 64, 1024),
        b_out.reshape(1, -1),
        ln_gain.reshape(1, -1),
        ln_bias.reshape(1, -1),
        head,
        query_feats,
        positive_rows,
        neg_ids,
    )
    z = (lax.axis_index("dp") // 2) % NZ
    return embedded, lax.dynamic_slice_in_dim(loss[0], z * 8, 4), head_grad


def solution(mesh):
    in_specs = (
        P(("dp", "fsdp"), None),
        P("fsdp", None),
        P(),
        P("fsdp", None),
        P(),
        P(),
        P(),
        P(),
        P(("dp", "fsdp"), None),
        P(("dp", "fsdp"), None),
        P(("dp", "fsdp"), None),
    )
    out_specs = (P(("dp", "fsdp"), None), P(("dp", "fsdp")), P("fsdp", None))
    return jax.shard_map(body, mesh=mesh, in_specs=in_specs, out_specs=out_specs, check_vma=False)
```

time: 865 us -> 121 us (0.14)
  waiting for transfers between devices: 795 us -> 0 us
  Pallas kernels: 0 us -> 108 us
  blocking collectives: 27.8 us -> 0 us
  matrix products: 17.3 us -> 0 us
  between operations: 13.9 us -> 0.7 us
  local copies, waits for them, and re-layouts: 2.83 us -> 11.7 us
    psum x1 -> x0, waiting for transfers between devices: 483 us -> none  [body(): summed_grad = lax.psum(term, ('dp', 'fsdp'))]
    all_gather x3 -> x0, waiting for transfers between devices: 311 us -> none  [the longest x1 128 us: body(): piece = lax.all_gather(group, 'dp', axis=0, tiled=True)]
    pallas_call x0 -> x1, Pallas kernels: none -> 108 us  [body(): pl.pallas_call(kernel, out_shape=(jax.ShapeDtypeStruct((4, 1024), BF16),...]
    all_gather x1 -> x0, blocking collectives: 27.8 us -> none  [body(): group = lax.all_gather(embedded, 'fsdp', axis=0, tiled=True)]
    dot_general x6 -> x0, matrix products: 17.3 us -> none  [the longest x1 10.2 us: body(): jnp.dot(columns, lax.all_gather(w_out, 'fsdp', axis=0, tiled=True), prefe...]
    unnamed x14 -> x24, local copies, waits for them, and re-layouts: 1.67 us -> 11.1 us
  transfers between devices with their start and end apart: 4 -> 0, of which waited for: 4 -> 0; matrix products, arithmetic and copies ran while one was open for 0% -> 0% of each run, Pallas kernels for 0% -> 0%
where the time goes in v1:
time: 121 us
  Pallas kernels  108 us (89%)
  local copies, waits for them, and re-layouts  11.7 us (10%)
    pallas_call x1, Pallas kernels, body(): pl.pallas_call(kernel, out_shape=(jax.ShapeDtypeStruct((4, 1024), BF16),...  108 us
    unnamed x24, local copies, waits for them, and re-layouts  11.1 us

profile of v1, /device:TPU:1, one launch (start us, length us, event | category | flops | bytes accessed | tf_op | source)
XLA Modules:
  0.0 120.7 jit_solution(1871626592533259543)
XLA Ops:
  0.7 0.0 copy-start
  0.7 1.6 %copy-done = bf16[1024,1024]{1,0:T(8,128)(2,1)S(1)} copy-done((bf16[1024,1024]{1,0:T(8,128)(2,1)S(1)}, bf16[1024,1024]{1,0:T(8,128)(2,1)}, u32[]{:S(2)}) %copy-start) | copy-done | bytes 2097176
  2.3 0.0 copy-start.1
  2.3 1.2 %copy-done.1 = bf16[512,1024]{1,0:T(8,128)(2,1)S(1)} copy-done((bf16[512,1024]{1,0:T(8,128)(2,1)S(1)}, bf16[512,1024]{1,0:T(8,128)(2,1)}, u32[]{:S(2)}) %copy-start.1) | copy-done | bytes 1048600
  3.5 0.0 copy-start.2
  3.5 1.0 copy-done.2
  4.5 0.0 copy-start.3
  4.5 1.0 copy-done.3
  5.6 0.0 copy-start.4
  5.6 0.7 copy-done.4
  6.3 0.0 copy-start.5
  6.3 0.7 copy-done.5
  7.0 0.0 copy-start.6
  7.0 0.7 copy-done.6
  7.7 0.0 copy-start.7
  7.7 0.7 copy-done.7
  8.3 0.0 copy-start.8
  8.4 0.7 copy-done.8
  9.0 0.7 copy-done.9
  9.7 0.7 copy-done.10
  10.4 108.2 %shard_map.130 = (bf16[4,1024]{1,0:T(4,128)(2,1)S(1)}, f32[8,128]{1,0:T(8,128)S(1)}, f32[128,1024]{1,0:T(8,128)S(1)}) custom-call(bf16[512,1024]{1,0:T(8,128)(2,1)S(1)} %copy-done.1, bf16[2,2,32,2048]{3,2,1,0:T(8,128)(2,1)S(1)} %bitcast.8, f32[1,2048]{1,0:T(1,128)S(1)} %bitcast.10, bf16[2,2,64,1024]{3,2,1,0:T(8,128)(2,1)S(1)} %bitcast.9, ...), custom_call_target="tpu_custom_call" | custom-call | tf_op jit(solution)/shard_map/pallas_call | solution.py:414
  118.7 0.6 dynamic-slice_bitcast_fusion
  119.3 0.6 copy.16
  119.9 0.8 copy.17
  (3 shorter events, 0.0 us)
Async XLA Ops:
  0.7 1.6 %copy-start = (bf16[1024,1024]{1,0:T(8,128)(2,1)S(1)}, bf16[1024,1024]{1,0:T(8,128)(2,1)}, u32[]{:S(2)}) copy-start(bf16[1024,1024]{1,0:T(8,128)(2,1)} %head.1) | copy-start | bytes 6291460
  2.3 1.2 %copy-start.1 = (bf16[512,1024]{1,0:T(8,128)(2,1)S(1)}, bf16[512,1024]{1,0:T(8,128)(2,1)}, u32[]{:S(2)}) copy-start(bf16[512,1024]{1,0:T(8,128)(2,1)} %tok.1) | copy-start | bytes 3145732
  3.5 1.0 copy-start.2
  4.5 1.0 copy-start.3
  5.6 0.7 copy-start.4
  6.3 0.7 copy-start.5
  7.0 0.7 copy-start.6
  7.7 0.7 copy-start.7
  8.3 0.7 copy-start.8
  9.0 0.7 copy-start.9
  9.7 0.7 copy-start.10

commit v2 on v1

v2 whole, which is shorter than its diff:
```python
import jax
import jax.numpy as jnp
from jax import lax
from jax.experimental import pallas as pl
from jax.experimental.pallas import tpu as pltpu
from jax.sharding import PartitionSpec as P

SEQ = 128
NX, NZ, NF, NPLANE = 4, 16, 8, 32
S1, S2 = 2, 2
score_scale = 0.5
eps = 1e-05
LOW = -3.0e38
MESH = pl.DeviceIdType.MESH
F32, BF16 = jnp.float32, jnp.bfloat16


def iota(shape, dim):
    return lax.broadcasted_iota(jnp.int32, shape, dim)


def dot(a, b, dims=(1, 0)):
    return lax.dot_general(
        a, b, (((dims[0],), (dims[1],)), ((), ())), preferred_element_type=F32
    )


def pick(mask):
    return mask.astype(F32).astype(BF16)


def take_all(ref, sem):
    pltpu.make_async_copy(ref, ref, sem).wait()


def kernel(
    tok_h, win, b_in_h, wout, b_out_h, gain_h, bias_h, head_h, feats_h, pos_h, ids_h,
    emb, loss, hg,
    tok, b_in, b_out, gain, bias, head, feats, pos, ids, inp,
    W1, W2, hid, summed, stg, qf16, idsb, pos16, r16, qfs, qfr, query, queryf, posf, idst, cT, rk,
    pk, stb, wr, gs, gr, rss, rsr, agr,
    crv, irv, srv, ssend, loc,
    zq, zi, pp, fq, rp, zs, fw, gx, zr, za, ga, psend,
):
    dp, f = lax.axis_index("dp"), lax.axis_index("fsdp")
    yl, z, c = dp // 32, (dp // 2) % NZ, dp % 2
    x, yh = f // 2, f % 2
    k = yl * 2 + c
    d = k * NF + f

    def chip(xx, hh, ll, cc):
        return (ll * 32 + z * 2 + cc, xx * 2 + hh)

    right, left = chip((x + 1) % NX, yh, yl, c), chip((x + 3) % NX, yh, yl, c)
    other, same = chip(x, 1 - yh, 1 - yl, c), chip(x, yh, 1 - yl, c)
    sibling = chip(x, yh, yl, 1 - c)

    def plane_peer(i):
        e = (d + i) % NPLANE
        return ((e // 16) * 32 + z * 2 + (e // 8) % 2, e % NF)

    def z_at(n):
        away = NZ // 2 + ((n + 1) // 2) * (2 * (n % 2) - 1)
        return (z + away) % NZ

    def z_peer(zz):
        return (yl * 32 + zz * 2 + c, f)

    def f_at(i):
        return (f + i) % NF

    def quarter_peer(i):
        e = (k + i) % 4
        return ((e // 2) * 32 + z * 2 + e % 2, f)

    def send(src, dst, ss, rs, to):
        copy = pltpu.make_async_remote_copy(
            src_ref=src, dst_ref=dst, send_sem=ss, recv_sem=rs, device_id=to, device_id_type=MESH
        )
        copy.start()
        return copy

    fetched = [
        pltpu.make_async_copy(a, b, inp.at[i])
        for i, (a, b) in enumerate(
            [(feats_h, feats), (pos_h, pos), (ids_h, ids), (tok_h, tok), (head_h, head),
             (b_in_h, b_in), (b_out_h, b_out), (gain_h, gain), (bias_h, bias)]
        )
    ]
    for copy in fetched:
        copy.start()

    barrier = pltpu.get_barrier_semaphore()

    @pl.loop(1, NPLANE)
    def _(i):
        pl.semaphore_signal(barrier, inc=1, device_id=plane_peer(i), device_id_type=MESH)

    @pl.loop(0, NZ - 1)
    def _(n):
        pl.semaphore_signal(barrier, inc=1, device_id=z_peer(z_at(n)), device_id_type=MESH)

    def spread(rows):
        for i in range(4):
            for j in range(4):
                stg[pl.ds(i * 4 + j, 1), :] = rows[i : i + 1, j * 256 : (j + 1) * 256]
        return stg[...].astype(BF16)

    for copy in fetched[:3]:
        copy.wait()
    qf16[z] = spread(feats[...].astype(F32))
    pos16[d] = spread(pos[...].astype(F32))
    posf[...] = jnp.zeros_like(posf)
    posf[0:4, :] = pos[...].astype(F32)
    idsb[z] = jnp.full((8, 128), -1, jnp.int32)
    idsb[z, 0:4, 0:64] = ids[...]

    pl.semaphore_wait(barrier, NPLANE - 1 + NZ - 1)

    col = (z + yl + yh) % 2
    xm, xp, xo = (x + 3) % NX, (x + 1) % NX, (x + 2) % NX
    zp, zm = z_peer((z + 1) % NZ), z_peer((z + NZ - 1) % NZ)
    far = chip(xo, yh, yl, c)

    def stage(s):
        if s < S1:
            return win, W1, pl.ds(s * (2048 // S1), 2048 // S1)
        return wout, W2, pl.ds((s - S1) * (1024 // S2), 1024 // S2)

    sent, leaving = [], []

    def out(s, n, ref, rs, to, src=None):
        sent.append(send(ref if src is None else src, ref, ssend.at[s, n], rs, to))

    def part(s, xx, hh, half):
        _, W, cols = stage(s)
        return W.at[xx, hh, c, half, :, cols]

    def ago(s):
        shard, _, cols = stage(s)
        ref, src = part(s, x, yh, col), shard.at[c, col, :, cols]
        out(s, 0, ref, crv.at[s, 0], right, src)
        out(s, 1, ref, crv.at[s, 1], left, src)
        out(s, 2, ref, crv.at[s, 3], other, src)
        out(s, 3, ref, crv.at[s, 2], far, src)

    def bgo(s):
        ref = part(s, x, 1 - yh, col)
        take_all(ref, crv.at[s, 3])
        out(s, 4, ref, crv.at[s, 4], right)
        out(s, 5, ref, crv.at[s, 5], left)
        out(s, 6, ref, irv.at[s, 1], same)
        ref = part(s, xm, yh, col)
        take_all(ref, crv.at[s, 0])
        out(s, 7, ref, irv.at[s, 0], same)
        ref = part(s, xp, yh, col)
        take_all(ref, crv.at[s, 1])
        out(s, 8, ref, irv.at[s, 0], zp)
        ref = part(s, xo, yh, col)
        take_all(ref, crv.at[s, 2])
        out(s, 9, ref, crv.at[s, 6], other)
        out(s, 10, ref, irv.at[s, 0], zm)

    def ego(s):
        ref = part(s, xm, 1 - yh, col)
        take_all(ref, crv.at[s, 4])
        out(s, 11, ref, irv.at[s, 1], zp)
        ref = part(s, xp, 1 - yh, col)
        take_all(ref, crv.at[s, 5])
        out(s, 12, ref, irv.at[s, 1], zm)
        ref = part(s, xo, 1 - yh, col)
        take_all(ref, crv.at[s, 6])
        out(s, 13, ref, irv.at[s, 1], same)

    def hgo(s):
        _, W, cols = stage(s)
        take_all(W.at[pl.ds(0, 3), yh, c, 1 - col, :, cols], irv.at[s, 0])
        out(s, 14, W.at[:, yh, c, :, :, cols], srv.at[s, 0], sibling)

    def igo(s):
        _, W, cols = stage(s)
        take_all(W.at[:, 1 - yh, c, 1 - col, :, cols], irv.at[s, 1])
        out(s, 15, W.at[:, 1 - yh, c, :, :, cols], srv.at[s, 1], sibling)

    def whole(s):
        _, W, cols = stage(s)
        take_all(W.at[:, yh, 1 - c, :, :, cols], srv.at[s, 0])
        take_all(W.at[:, 1 - yh, 1 - c, :, :, cols], srv.at[s, 1])

    def compute(s):
        if s < S1:

            @pl.loop(0, 8 // S1)
            def _(n):
                at = pl.ds(pl.multiple_of(s * (2048 // S1) + n * 256, 256), 256)
                w = W1[:, :, :, :, :, at].reshape(1024, 256)
                v = dot(tok[...], w) + b_in[:, at]
                g = 0.5 * v * (1.0 + jnp.tanh(0.7978845608 * (v + 0.044715 * (v * v * v))))
                hid[:, at] = g.astype(BF16)
        else:

            @pl.loop(0, 4 // S2)
            def _(n):
                at = pl.ds(pl.multiple_of((s - S1) * (1024 // S2) + n * 256, 256), 256)
                w = W2[:, :, :, :, :, at].reshape(2048, 256)
                summed[:, at] = tok[:, at].astype(F32) + dot(hid[...], w) + b_out[:, at]

    ago(0)
    ago(1)
    keep1 = pltpu.make_async_copy(win.at[c], W1.at[x, yh, c], loc.at[0])
    keep2 = pltpu.make_async_copy(wout.at[c], W2.at[x, yh, c], loc.at[1])
    keep1.start()
    keep2.start()

    @pl.loop(0, NZ - 1)
    def _(n):
        to = z_peer(z_at(n))
        send(qf16.at[z], qf16.at[z], psend.at[0], zq.at[0], to)
        send(idsb.at[z], idsb.at[z], psend.at[1], zi.at[0], to)

    leaving.append((qf16.at[pl.ds(0, NZ - 1)], psend.at[0]))
    leaving.append((idsb.at[pl.ds(0, NZ - 1)], psend.at[1]))

    keep1.wait()
    keep2.wait()
    for copy in fetched[3:]:
        copy.wait()

    def prep_column():
        take_all(qf16.at[pl.ds(0, NZ - 1)], zq.at[0])
        flat = qf16[...].reshape(NZ * 16, 256)
        for j in range(4):
            sel = pick(iota((64, 256), 1) == 4 * iota((64, 256), 0) + j)
            rows = dot(sel, flat).astype(BF16)
            qfs[2 * j] = rows[:, :128]
            qfs[2 * j + 1] = rows[:, 128:]
        qfr[f] = qfs[f]

    def prep_query():
        flat = qf16[...].reshape(NZ * 16, 256)
        total_q = jnp.zeros((128, 1024), F32)
        m = iota((128, 256), 0)
        for j in range(4):
            sel = pick((iota((128, 256), 1) == (m // 8) * 16 + (m % 8) * 4 + j) & (m % 8 < 4))
            rows = dot(sel, flat).astype(BF16)
            total_q = total_q + dot(rows, head[j * 256 : (j + 1) * 256, :])
        query[...] = total_q.astype(BF16)
        queryf[...] = query[...].astype(F32)


    def prep_count():
        take_all(idsb.at[pl.ds(0, NZ - 1)], zi.at[0])
        idst[...] = jnp.transpose(idsb[...].reshape(128, 128).astype(F32))
        pi = iota((128, 1), 0)
        pid = (((pi // 64) * 32 + z * 2 + (pi // 32) % 2) * NF + (pi // 4) % NF) * 4 + pi % 4
        pid = pid.astype(F32)
        cT[...] = lax.fori_loop(
            0, 64,
            lambda t, a: a + (idst[pl.ds(t, 1), :] == pid).astype(F32),
            jnp.zeros((128, 128), F32),
        )


    extra = {1: prep_column, 3: prep_query, 4: prep_count}
    NS = S1 + S2
    for tick in range(1, NS + 4):
        if tick <= NS:
            bgo(tick - 1)
            if tick + 1 < NS:
                ago(tick + 1)
        if 0 <= tick - 2 < NS:
            ego(tick - 2)
            hgo(tick - 2)
        if 0 <= tick - 3 < NS:
            igo(tick - 3)
        if tick in extra:
            extra[tick]()
        if 0 <= tick - 4 < NS:
            whole(tick - 4)
            compute(tick - 4)

    rows = []
    for i in range(4):
        v = summed[i * SEQ : (i + 1) * SEQ, :]
        center = v - jnp.mean(v, axis=-1, keepdims=True)
        spread_ = jnp.mean(center * center, axis=-1, keepdims=True)
        normed = center * lax.rsqrt(spread_ + eps)
        rows.append(jnp.sum(normed, axis=0, keepdims=True) * (1.0 / SEQ) * gain[...] + bias[...])
    pooled = jnp.concatenate(rows, axis=0)
    emb[...] = pooled.astype(BF16)
    r16[d] = spread(pooled)

    @pl.loop(1, NPLANE)
    def _(i):
        send(r16.at[d], r16.at[d], psend.at[4], rp.at[0], plane_peer(i))

    leaving.append((r16.at[pl.ds(0, NPLANE - 1)], psend.at[4]))

    lane = iota((1, 128), 1)
    mine = (lane // 8 == z) & (lane % 8 < 4)
    s_col = score_scale * jnp.sum(
        queryf[pl.ds(pl.multiple_of(z * 8, 8), 8), :] * posf[...], axis=-1, keepdims=True
    )
    s_pos = jnp.sum(
        jnp.where(iota((8, 128), 1) == z * 8 + iota((8, 128), 0), s_col, 0.0), axis=0, keepdims=True
    )

    take_all(r16.at[pl.ds(0, NPLANE - 1)], rp.at[0])
    flat_r = r16[...].reshape(NPLANE * 16, 256)
    s = jnp.zeros((128, 128), F32)
    for j in range(4):
        sel = pick(iota((128, 512), 1) == 4 * iota((128, 512), 0) + j)
        rows = dot(sel, flat_r).astype(BF16)
        rk[j] = rows
        s = s + dot(rows, query[:, j * 256 : (j + 1) * 256], (1, 1))
    s = s * score_scale
    count = cT[...]
    listed = count > 0.0
    high = jnp.max(jnp.where(listed, s, LOW), axis=0, keepdims=True)
    part = jnp.sum(
        jnp.where(listed, count * jnp.exp(jnp.where(listed, s - high, 0.0)), 0.0), axis=0, keepdims=True
    )
    high2 = jnp.where(mine, jnp.maximum(high, s_pos), high)
    part2 = part * jnp.exp(high - high2) + jnp.where(mine, jnp.exp(s_pos - high2), 0.0)
    r8 = iota((8, 128), 0)
    stb[z] = jnp.where(r8 == 0, high2, jnp.where(r8 == 1, part2, 0.0))

    @pl.loop(0, NZ - 1)
    def _(n):
        send(stb.at[z], stb.at[z], psend.at[5], zs.at[0], z_peer(z_at(n)))

    leaving.append((stb.at[pl.ds(0, NZ - 1)], psend.at[5]))

    @pl.loop(1, NF)
    def _(i):
        to = f_at(i)
        send(qfs.at[to], qfr.at[f], psend.at[2], fq.at[0], (dp, to))

    leaving.append((qfr.at[pl.ds(0, NF - 1)], psend.at[2]))

    @pl.loop(1, NPLANE)
    def _(i):
        send(pos16.at[d], pos16.at[d], psend.at[3], pp.at[0], plane_peer(i))

    leaving.append((pos16.at[pl.ds(0, NPLANE - 1)], psend.at[3]))

    take_all(stb.at[pl.ds(0, NZ - 1)], zs.at[0])
    stats = stb[...]
    highs, parts = stats[:, 0, :], stats[:, 1, :]
    top = jnp.max(highs, axis=0, keepdims=True)
    total = top + jnp.log(jnp.sum(parts * jnp.exp(highs - top), axis=0, keepdims=True))
    loss[...] = jnp.where(r8 == 0, jnp.where(mine, total - s_pos, 0.0), 0.0)
    coeff = jnp.where(mine, jnp.exp(jnp.where(mine, s_pos - total, 0.0)) - 1.0, 0.0)
    w = jnp.exp(jnp.where(listed, s - total, 0.0)).astype(BF16).astype(F32)
    w = jnp.where(listed, count * w, 0.0).astype(BF16)
    j64 = iota((64, 128), 0)
    wr[f, 0:64, :] = dot(pick(iota((64, 128), 1) == (j64 // 4) * 8 + j64 % 4), w, (1, 1)).astype(BF16)
    c0 = coeff.astype(BF16).astype(F32)
    c1 = (coeff - c0).astype(BF16).astype(F32)
    c2 = coeff - c0 - c1
    r16i = iota((16, 128), 0)
    wr[f, 64:80, :] = jnp.where(
        r16i == 0, c0, jnp.where(r16i == 1, c1, jnp.where(r16i == 2, c2, 0.0))
    ).astype(BF16)

    @pl.loop(1, NF)
    def _(i):
        send(wr.at[f], wr.at[f], psend.at[6], fw.at[0], (dp, f_at(i)))

    leaving.append((wr.at[pl.ds(0, NF - 1)], psend.at[6]))

    take_all(pos16.at[pl.ds(0, NPLANE - 1)], pp.at[0])
    flat_p = pos16[...].reshape(NPLANE * 16, 256)
    for j in range(4):
        sel = pick(iota((128, 512), 1) == 4 * iota((128, 512), 0) + j)
        pk[j] = dot(sel, flat_p).astype(BF16)
    take_all(qfr.at[pl.ds(0, NF - 1)], fq.at[0])
    slices = qfr[...].reshape(NF * 64, 128)
    g32 = iota((32, 512), 0)
    group_q = dot(pick(iota((32, 512), 1) == (g32 // 4) * 64 + z * 4 + g32 % 4), slices)

    take_all(wr.at[pl.ds(0, NF - 1)], fw.at[0])
    g_part = dot(slices, wr[:, 0:64, :].reshape(NF * 64, 128), (0, 0)).astype(BF16)
    e32, l32 = iota((32, 128), 0), iota((32, 128), 1)
    expand = pick((l32 // 16 == e32 // 4) & (l32 % 16 < 3))
    co = dot(expand, wr[:, 64:80, :].reshape(128, 128))
    co = jnp.sum(jnp.where(l32 == z * 8 + e32 % 4, co, 0.0), axis=1, keepdims=True)
    g_pos = (group_q * co).astype(BF16)
    shift = pick(l32 == k * 32 + e32)
    g_pos = dot(g_pos, shift, (0, 0)).astype(BF16)
    for e in range(4):
        gs[e, 0:32, :] = g_part[e * 32 : e * 32 + 32, :]
        gs[e, 32:64, :] = g_pos[e * 32 : e * 32 + 32, :]
    gr[k] = gs[k]

    @pl.loop(1, 4)
    def _(i):
        to = (k + i) % 4
        send(gs.at[to], gr.at[k], psend.at[7], gx.at[0], quarter_peer(i))

    leaving.append((gr.at[pl.ds(0, 3)], psend.at[7]))

    take_all(gr.at[pl.ds(0, 3)], gx.at[0])
    g_all = jnp.sum(gr[...].astype(F32), axis=0).astype(BF16)
    for e in range(4):
        term = score_scale * (dot(g_all[0:32, :], rk[e]) + dot(g_all[32:64, :], pk[e]))
        term = term.astype(BF16)
        for t in range(4):
            rss[e * 2 + t % 2 + 8 * (t // 2)] = term[(t // 2) * 16 : (t // 2) * 16 + 16, (t % 2) * 128 : (t % 2) * 128 + 128]
    rsr[z] = rss[z]

    @pl.loop(0, NZ - 1)
    def _(n):
        to = z_at(n)
        send(rss.at[to], rsr.at[z], psend.at[8], zr.at[0], z_peer(to))

    leaving.append((rsr.at[pl.ds(0, NZ - 1)], psend.at[8]))

    take_all(rsr.at[pl.ds(0, NZ - 1)], zr.at[0])
    agr[k, z] = jnp.sum(rsr[...].astype(F32), axis=0).astype(BF16)

    @pl.loop(0, NZ - 1)
    def _(n):
        send(agr.at[k, z], agr.at[k, z], psend.at[9], za.at[0], z_peer(z_at(n)))

    leaving.append((agr.at[0, pl.ds(0, NZ - 1)], psend.at[9]))

    take_all(agr.at[k, pl.ds(0, NZ - 1)], za.at[0])

    @pl.loop(1, 4)
    def _(i):
        send(agr.at[k], agr.at[k], psend.at[10], ga.at[0], quarter_peer(i))

    leaving.append((agr.at[pl.ds(0, 3)], psend.at[10]))

    take_all(agr.at[pl.ds(0, 3)], ga.at[0])
    for e in range(4):
        for t in range(NZ):
            row, at = e * 32 + (t // 8) * 16, (t % 8) * 128
            hg[row : row + 16, at : at + 128] = agr[e, t].astype(F32)

    for copy in sent:
        copy.wait_send()
    for ref, sem in leaving:
        take_all(ref, sem)


def body(
    tokens, w_in, b_in, w_out, b_out, ln_gain, ln_bias, head, query_feats, positive_rows, neg_ids
):
    vmem = pl.BlockSpec(memory_space=pltpu.VMEM)
    V, S = pltpu.VMEM, pltpu.SemaphoreType.DMA
    embedded, loss, head_grad = pl.pallas_call(
        kernel,
        out_shape=(
            jax.ShapeDtypeStruct((4, 1024), BF16),
            jax.ShapeDtypeStruct((8, 128), F32),
            jax.ShapeDtypeStruct((128, 1024), F32),
        ),
        in_specs=[pl.BlockSpec(memory_space=pl.ANY)] * 11,
        out_specs=(vmem,) * 3,
        scratch_shapes=[
            V((512, 1024), BF16),
            V((1, 2048), F32),
            V((1, 1024), F32),
            V((1, 1024), F32),
            V((1, 1024), F32),
            V((1024, 1024), BF16),
            V((4, 1024), BF16),
            V((4, 1024), BF16),
            V((4, 64), jnp.int32),
            S((9,)),
            V((4, 2, 2, 2, 32, 2048), BF16),
            V((4, 2, 2, 2, 64, 1024), BF16),
            V((512, 2048), BF16),
            V((512, 1024), F32),
            V((16, 256), F32),
            V((NZ, 16, 256), BF16),
            V((NZ, 8, 128), jnp.int32),
            V((NPLANE, 16, 256), BF16),
            V((NPLANE, 16, 256), BF16),
            V((NF, 64, 128), BF16),
            V((NF, 64, 128), BF16),
            V((128, 1024), BF16),
            V((128, 1024), F32),
            V((8, 1024), F32),
            V((128, 128), F32),
            V((128, 128), F32),
            V((4, 128, 256), BF16),
            V((4, 128, 256), BF16),
            V((NZ, 8, 128), F32),
            V((NF, 80, 128), BF16),
            V((4, 64, 128), BF16),
            V((4, 64, 128), BF16),
            V((NZ, 16, 128), BF16),
            V((NZ, 16, 128), BF16),
            V((4, NZ, 16, 128), BF16),
        ]
        + [S((S1 + S2, 7)), S((S1 + S2, 2)), S((S1 + S2, 2)), S((S1 + S2, 16)), S((2,))]
        + [S((1,))] * 11
        + [S((11,))],
        compiler_params=pltpu.CompilerParams(
            collective_id=0, has_side_effects=True, vmem_limit_bytes=60 << 20
        ),
    )(
        tokens,
        w_in.reshape(2, 2, 32, 2048),
        b_in.reshape(1, -1),
        w_out.reshape(2, 2, 64, 1024),
        b_out.reshape(1, -1),
        ln_gain.reshape(1, -1),
        ln_bias.reshape(1, -1),
        head,
        query_feats,
        positive_rows,
        neg_ids,
    )
    z = (lax.axis_index("dp") // 2) % NZ
    return embedded, lax.dynamic_slice_in_dim(loss[0], z * 8, 4), head_grad


def solution(mesh):
    in_specs = (
        P(("dp", "fsdp"), None),
        P("fsdp", None),
        P(),
        P("fsdp", None),
        P(),
        P(),
        P(),
        P(),
        P(("dp", "fsdp"), None),
        P(("dp", "fsdp"), None),
        P(("dp", "fsdp"), None),
    )
    out_specs = (P(("dp", "fsdp"), None), P(("dp", "fsdp")), P("fsdp", None))
    return jax.shard_map(body, mesh=mesh, in_specs=in_specs, out_specs=out_specs, check_vma=False)
```

time: 121 us -> 98.5 us (0.81)
  Pallas kernels: 108 us -> 93.1 us
  local copies, waits for them, and re-layouts: 11.7 us -> 4.45 us
    pallas_call x1, Pallas kernels: 108 us -> 93.1 us  [body(): pl.pallas_call(kernel, out_shape=(jax.ShapeDtypeStruct((4, 1024), BF16),...]
    unnamed x24 -> x2, local copies, waits for them, and re-layouts: 11.1 us -> 3.18 us
where the time goes in v2:
time: 98.5 us; the launch traced here: 98.2 us
  Pallas kernels  93.1 us (95%)
  local copies, waits for them, and re-layouts  4.45 us (5%)
    pallas_call x1, Pallas kernels, body(): pl.pallas_call(kernel, out_shape=(jax.ShapeDtypeStruct((4, 1024), BF16),...  93.1 us
    unnamed x2, local copies, waits for them, and re-layouts  3.18 us

profile of v2, /device:TPU:1, one launch (start us, length us, event | category | flops | bytes accessed | tf_op | source)
XLA Modules:
  0.0 98.2 jit_solution(11408539833255573295)
XLA Ops:
  0.7 93.1 %shard_map.130 = (bf16[4,1024]{1,0:T(4,128)(2,1)}, f32[8,128]{1,0:T(8,128)}, f32[128,1024]{1,0:T(8,128)}) custom-call(bf16[512,1024]{1,0:T(8,128)(2,1)} %tok_h.1, bf16[2,2,32,2048]{3,2,1,0:T(8,128)(2,1)} %bitcast.8, f32[1,2048]{1,0:T(1,128)} %bitcast.10, bf16[2,2,64,1024]{3,2,1,0:T(8,128)(2,1)} %bitcast.9, f32[1,1024]{1,0:T(1,128)} %bitcast.11, ...), custom_call_target="tpu_custom_call" | custom-call | tf_op jit(solution)/shard_map/pallas_call | solution.py:453
  93.8 0.7 slice.3
  94.5 0.6 dynamic-slice_bitcast_fusion
  95.1 1.3 %copy.16 = bf16[4,1024]{1,0:T(4,128)(2,1)} copy(bf16[4,1024]{1,0:T(4,128)(2,1)} %get-tuple-element.12) | data formatting | bytes 16384
  96.4 1.9 %copy.17 = f32[128,1024]{1,0:T(8,128)} copy(f32[128,1024]{1,0:T(8,128)} %get-tuple-element.14) | data formatting | bytes 1048576

commit v3 on v2

--- a/solution.py
+++ b/solution.py
@@ -7,11 +7,13 @@
 
 SEQ = 128
 NX, NZ, NF, NPLANE = 4, 16, 8, 32
-S1, S2 = 2, 2
+WIDTHS1, WIDTHS2 = (1024, 1024), (512, 512)
+NS = len(WIDTHS1) + len(WIDTHS2)
 score_scale = 0.5
 eps = 1e-05
 LOW = -3.0e38
 MESH = pl.DeviceIdType.MESH
+div, rem = lax.div, lax.rem
 F32, BF16 = jnp.float32, jnp.bfloat16
 
 
@@ -25,6 +27,14 @@
     )
 
 
+def hi(a, n):
+    return lax.shift_right_logical(a, jnp.full(a.shape, n.bit_length() - 1, jnp.int32))
+
+
+def lo(a, n):
+    return a & (n - 1)
+
+
 def pick(mask):
     return mask.astype(F32).astype(BF16)
 
@@ -35,43 +45,42 @@
 
 def kernel(
     tok_h, win, b_in_h, wout, b_out_h, gain_h, bias_h, head_h, feats_h, pos_h, ids_h,
-    emb, loss, hg,
+    emb, loss, grads,
     tok, b_in, b_out, gain, bias, head, feats, pos, ids, inp,
     W1, W2, hid, summed, stg, qf16, idsb, pos16, r16, qfs, qfr, query, queryf, posf, idst, cT, rk,
-    pk, stb, wr, gs, gr, rss, rsr, agr,
+    pk, selr, stb, wr, gs, gr, rss, rsr, agr,
     crv, irv, srv, ssend, loc,
     zq, zi, pp, fq, rp, zs, fw, gx, zr, za, ga, psend,
 ):
     dp, f = lax.axis_index("dp"), lax.axis_index("fsdp")
-    yl, z, c = dp // 32, (dp // 2) % NZ, dp % 2
-    x, yh = f // 2, f % 2
+    yl, z, c = div(dp, 32), rem(div(dp, 2), NZ), rem(dp, 2)
+    x, yh = div(f, 2), rem(f, 2)
     k = yl * 2 + c
     d = k * NF + f
 
-    def chip(xx, hh, ll, cc):
-        return (ll * 32 + z * 2 + cc, xx * 2 + hh)
-
-    right, left = chip((x + 1) % NX, yh, yl, c), chip((x + 3) % NX, yh, yl, c)
-    other, same = chip(x, 1 - yh, 1 - yl, c), chip(x, yh, 1 - yl, c)
-    sibling = chip(x, yh, yl, 1 - c)
-
-    def plane_peer(i):
-        e = (d + i) % NPLANE
-        return ((e // 16) * 32 + z * 2 + (e // 8) % 2, e % NF)
-
-    def z_at(n):
-        away = NZ // 2 + ((n + 1) // 2) * (2 * (n % 2) - 1)
-        return (z + away) % NZ
-
-    def z_peer(zz):
-        return (yl * 32 + zz * 2 + c, f)
-
-    def f_at(i):
-        return (f + i) % NF
-
-    def quarter_peer(i):
-        e = (k + i) % 4
-        return ((e // 2) * 32 + z * 2 + e % 2, f)
+    y = 2 * yh + yl
+    xs = [x] + [rem(x + i, NX) for i in range(1, NX)]
+    zz = [z] + [rem(z + i, NZ) for i in range(1, NZ)]
+    yhs, yls = [yh], [yl]
+    for i in range(1, 4):
+        v = rem(y + i, 4)
+        yhs.append(div(v, 2))
+        yls.append(rem(v, 2))
+    cs = [c, 1 - c]
+    dps = [[v * 32 + z * 2 + w for w in cs] for v in yls]
+    fs = [[v * 2 + w for w in yhs] for v in xs]
+    plane = [
+        (dps[j][w], fs[i][j]) for i in (2, 3, 1, 0) for j in (2, 3, 1, 0) for w in (1, 0) if i or j or w
+    ]
+    column = [(zz[i], (yl * 32 + zz[i] * 2 + c, f)) for i in (8, 9, 7, 10, 6, 11, 5, 12, 4, 13, 3, 14, 2, 15, 1)]
+    row = [xs[i] * 2 + v for i in (2, 3, 1, 0) for v in (1 - yh, yh)][:-1]
+    quarter = [
+        (v * 2 + w, (v * 32 + z * 2 + w, f)) for v, w in ((1 - yl, 1 - c), (1 - yl, c), (yl, 1 - c))
+    ]
+    right, left, far = (dp, fs[1][0]), (dp, fs[3][0]), (dp, fs[2][0])
+    other, same = ((1 - yl) * 32 + z * 2 + c, x * 2 + 1 - yh), ((1 - yl) * 32 + z * 2 + c, f)
+    sibling = (dps[0][1], f)
+    zp, zm = column[-1][1], column[-2][1]
 
     def send(src, dst, ss, rs, to):
         copy = pltpu.make_async_remote_copy(
@@ -79,6 +88,14 @@
         )
         copy.start()
         return copy
+
+    barrier = pltpu.get_barrier_semaphore()
+
+    for _, to in column:
+        pl.semaphore_signal(barrier, inc=1, device_id=to, device_id_type=MESH)
+
+    for to in plane:
+        pl.semaphore_signal(barrier, inc=1, device_id=to, device_id_type=MESH)
 
     fetched = [
         pltpu.make_async_copy(a, b, inp.at[i])
@@ -90,16 +107,6 @@
     for copy in fetched:
         copy.start()
 
-    barrier = pltpu.get_barrier_semaphore()
-
-    @pl.loop(1, NPLANE)
-    def _(i):
-        pl.semaphore_signal(barrier, inc=1, device_id=plane_peer(i), device_id_type=MESH)
-
-    @pl.loop(0, NZ - 1)
-    def _(n):
-        pl.semaphore_signal(barrier, inc=1, device_id=z_peer(z_at(n)), device_id_type=MESH)
-
     def spread(rows):
         for i in range(4):
             for j in range(4):
@@ -117,15 +124,14 @@
 
     pl.semaphore_wait(barrier, NPLANE - 1 + NZ - 1)
 
-    col = (z + yl + yh) % 2
-    xm, xp, xo = (x + 3) % NX, (x + 1) % NX, (x + 2) % NX
-    zp, zm = z_peer((z + 1) % NZ), z_peer((z + NZ - 1) % NZ)
-    far = chip(xo, yh, yl, c)
+    col = rem(z + yl + yh, 2)
+    xm, xp, xo = xs[3], xs[1], xs[2]
 
     def stage(s):
-        if s < S1:
-            return win, W1, pl.ds(s * (2048 // S1), 2048 // S1)
-        return wout, W2, pl.ds((s - S1) * (1024 // S2), 1024 // S2)
+        if s < len(WIDTHS1):
+            return win, W1, pl.ds(sum(WIDTHS1[:s]), WIDTHS1[s])
+        s -= len(WIDTHS1)
+        return wout, W2, pl.ds(sum(WIDTHS2[:s]), WIDTHS2[s])
 
     sent, leaving = [], []
 
@@ -188,21 +194,17 @@
         take_all(W.at[:, 1 - yh, 1 - c, :, :, cols], srv.at[s, 1])
 
     def compute(s):
-        if s < S1:
-
-            @pl.loop(0, 8 // S1)
-            def _(n):
-                at = pl.ds(pl.multiple_of(s * (2048 // S1) + n * 256, 256), 256)
-                w = W1[:, :, :, :, :, at].reshape(1024, 256)
+        _, W, cols = stage(s)
+
+        @pl.loop(0, cols.size // 256)
+        def _(n):
+            at = pl.ds(pl.multiple_of(cols.start + n * 256, 256), 256)
+            w = W[:, :, :, :, :, at].reshape(-1, 256)
+            if W is W1:
                 v = dot(tok[...], w) + b_in[:, at]
                 g = 0.5 * v * (1.0 + jnp.tanh(0.7978845608 * (v + 0.044715 * (v * v * v))))
                 hid[:, at] = g.astype(BF16)
-        else:
-
-            @pl.loop(0, 4 // S2)
-            def _(n):
-                at = pl.ds(pl.multiple_of((s - S1) * (1024 // S2) + n * 256, 256), 256)
-                w = W2[:, :, :, :, :, at].reshape(2048, 256)
+            else:
                 summed[:, at] = tok[:, at].astype(F32) + dot(hid[...], w) + b_out[:, at]
 
     ago(0)
@@ -212,14 +214,15 @@
     keep1.start()
     keep2.start()
 
-    @pl.loop(0, NZ - 1)
-    def _(n):
-        to = z_peer(z_at(n))
+    for _, to in column:
         send(qf16.at[z], qf16.at[z], psend.at[0], zq.at[0], to)
         send(idsb.at[z], idsb.at[z], psend.at[1], zi.at[0], to)
 
     leaving.append((qf16.at[pl.ds(0, NZ - 1)], psend.at[0]))
     leaving.append((idsb.at[pl.ds(0, NZ - 1)], psend.at[1]))
+
+    for j in range(4):
+        selr[j] = pick(iota((128, 512), 1) == 4 * iota((128, 1), 0) + j)
 
     keep1.wait()
     keep2.wait()
@@ -227,21 +230,22 @@
         copy.wait()
 
     def prep_column():
-        take_all(qf16.at[pl.ds(0, NZ - 1)], zq.at[0])
         flat = qf16[...].reshape(NZ * 16, 256)
         for j in range(4):
-            sel = pick(iota((64, 256), 1) == 4 * iota((64, 256), 0) + j)
+            sel = pick(iota((64, 256), 1) == 4 * iota((64, 1), 0) + j)
             rows = dot(sel, flat).astype(BF16)
             qfs[2 * j] = rows[:, :128]
             qfs[2 * j + 1] = rows[:, 128:]
         qfr[f] = qfs[f]
 
     def prep_query():
+        take_all(qf16.at[pl.ds(0, NZ - 1)], zq.at[0])
         flat = qf16[...].reshape(NZ * 16, 256)
         total_q = jnp.zeros((128, 1024), F32)
-        m = iota((128, 256), 0)
+        m = iota((128, 1), 0)
+        at = jnp.where(lo(m, 8) < 4, hi(m, 8) * 16 + lo(m, 8) * 4, -8)
         for j in range(4):
-            sel = pick((iota((128, 256), 1) == (m // 8) * 16 + (m % 8) * 4 + j) & (m % 8 < 4))
+            sel = pick(iota((128, 256), 1) == at + j)
             rows = dot(sel, flat).astype(BF16)
             total_q = total_q + dot(rows, head[j * 256 : (j + 1) * 256, :])
         query[...] = total_q.astype(BF16)
@@ -252,7 +256,7 @@
         take_all(idsb.at[pl.ds(0, NZ - 1)], zi.at[0])
         idst[...] = jnp.transpose(idsb[...].reshape(128, 128).astype(F32))
         pi = iota((128, 1), 0)
-        pid = (((pi // 64) * 32 + z * 2 + (pi // 32) % 2) * NF + (pi // 4) % NF) * 4 + pi % 4
+        pid = ((hi(pi, 64) * 32 + z * 2 + lo(hi(pi, 32), 2)) * NF + lo(hi(pi, 4), NF)) * 4 + lo(pi, 4)
         pid = pid.astype(F32)
         cT[...] = lax.fori_loop(
             0, 64,
@@ -261,8 +265,7 @@
         )
 
 
-    extra = {1: prep_column, 3: prep_query, 4: prep_count}
-    NS = S1 + S2
+    extra = {3: prep_query}
     for tick in range(1, NS + 4):
         if tick <= NS:
             bgo(tick - 1)
@@ -290,14 +293,15 @@
     emb[...] = pooled.astype(BF16)
     r16[d] = spread(pooled)
 
-    @pl.loop(1, NPLANE)
-    def _(i):
-        send(r16.at[d], r16.at[d], psend.at[4], rp.at[0], plane_peer(i))
+    for to in plane:
+        send(r16.at[d], r16.at[d], psend.at[4], rp.at[0], to)
 
     leaving.append((r16.at[pl.ds(0, NPLANE - 1)], psend.at[4]))
 
+    prep_count()
+    prep_column()
     lane = iota((1, 128), 1)
-    mine = (lane // 8 == z) & (lane % 8 < 4)
+    mine = (hi(lane, 8) == z) & (lo(lane, 8) < 4)
     s_col = score_scale * jnp.sum(
         queryf[pl.ds(pl.multiple_of(z * 8, 8), 8), :] * posf[...], axis=-1, keepdims=True
     )
@@ -309,8 +313,7 @@
     flat_r = r16[...].reshape(NPLANE * 16, 256)
     s = jnp.zeros((128, 128), F32)
     for j in range(4):
-        sel = pick(iota((128, 512), 1) == 4 * iota((128, 512), 0) + j)
-        rows = dot(sel, flat_r).astype(BF16)
+        rows = dot(selr[j], flat_r).astype(BF16)
         rk[j] = rows
         s = s + dot(rows, query[:, j * 256 : (j + 1) * 256], (1, 1))
     s = s * score_scale
@@ -325,24 +328,23 @@
     r8 = iota((8, 128), 0)
     stb[z] = jnp.where(r8 == 0, high2, jnp.where(r8 == 1, part2, 0.0))
 
-    @pl.loop(0, NZ - 1)
-    def _(n):
-        send(stb.at[z], stb.at[z], psend.at[5], zs.at[0], z_peer(z_at(n)))
+    for _, to in column:
+        send(stb.at[z], stb.at[z], psend.at[5], zs.at[0], to)
 
     leaving.append((stb.at[pl.ds(0, NZ - 1)], psend.at[5]))
 
-    @pl.loop(1, NF)
-    def _(i):
-        to = f_at(i)
+    for to in row:
         send(qfs.at[to], qfr.at[f], psend.at[2], fq.at[0], (dp, to))
 
     leaving.append((qfr.at[pl.ds(0, NF - 1)], psend.at[2]))
 
-    @pl.loop(1, NPLANE)
-    def _(i):
-        send(pos16.at[d], pos16.at[d], psend.at[3], pp.at[0], plane_peer(i))
+    for to in plane:
+        send(pos16.at[d], pos16.at[d], psend.at[3], pp.at[0], to)
 
     leaving.append((pos16.at[pl.ds(0, NPLANE - 1)], psend.at[3]))
+
+    j64 = iota((64, 1), 0)
+    squeeze = pick(iota((64, 128), 1) == hi(j64, 4) * 8 + lo(j64, 4))
 
     take_all(stb.at[pl.ds(0, NZ - 1)], zs.at[0])
     stats = stb[...]
@@ -353,8 +355,7 @@
     coeff = jnp.where(mine, jnp.exp(jnp.where(mine, s_pos - total, 0.0)) - 1.0, 0.0)
     w = jnp.exp(jnp.where(listed, s - total, 0.0)).astype(BF16).astype(F32)
     w = jnp.where(listed, count * w, 0.0).astype(BF16)
-    j64 = iota((64, 128), 0)
-    wr[f, 0:64, :] = dot(pick(iota((64, 128), 1) == (j64 // 4) * 8 + j64 % 4), w, (1, 1)).astype(BF16)
+    wr[f, 0:64, :] = dot(squeeze, w, (1, 1)).astype(BF16)
     c0 = coeff.astype(BF16).astype(F32)
     c1 = (coeff - c0).astype(BF16).astype(F32)
     c2 = coeff - c0 - c1
@@ -363,40 +364,36 @@
         r16i == 0, c0, jnp.where(r16i == 1, c1, jnp.where(r16i == 2, c2, 0.0))
     ).astype(BF16)
 
-    @pl.loop(1, NF)
-    def _(i):
-        send(wr.at[f], wr.at[f], psend.at[6], fw.at[0], (dp, f_at(i)))
+    for to in row:
+        send(wr.at[f], wr.at[f], psend.at[6], fw.at[0], (dp, to))
 
     leaving.append((wr.at[pl.ds(0, NF - 1)], psend.at[6]))
 
     take_all(pos16.at[pl.ds(0, NPLANE - 1)], pp.at[0])
     flat_p = pos16[...].reshape(NPLANE * 16, 256)
     for j in range(4):
-        sel = pick(iota((128, 512), 1) == 4 * iota((128, 512), 0) + j)
-        pk[j] = dot(sel, flat_p).astype(BF16)
+        pk[j] = dot(selr[j], flat_p).astype(BF16)
     take_all(qfr.at[pl.ds(0, NF - 1)], fq.at[0])
     slices = qfr[...].reshape(NF * 64, 128)
-    g32 = iota((32, 512), 0)
-    group_q = dot(pick(iota((32, 512), 1) == (g32 // 4) * 64 + z * 4 + g32 % 4), slices)
+    e32, l32 = iota((32, 1), 0), iota((32, 128), 1)
+    group_q = dot(pick(iota((32, 512), 1) == hi(e32, 4) * 64 + z * 4 + lo(e32, 4)), slices)
+    expand = pick((hi(l32, 16) == hi(e32, 4)) & (lo(l32, 16) < 3))
+    own_lane = l32 == z * 8 + lo(e32, 4)
+    shift = pick(l32 == k * 32 + e32)
 
     take_all(wr.at[pl.ds(0, NF - 1)], fw.at[0])
     g_part = dot(slices, wr[:, 0:64, :].reshape(NF * 64, 128), (0, 0)).astype(BF16)
-    e32, l32 = iota((32, 128), 0), iota((32, 128), 1)
-    expand = pick((l32 // 16 == e32 // 4) & (l32 % 16 < 3))
     co = dot(expand, wr[:, 64:80, :].reshape(128, 128))
-    co = jnp.sum(jnp.where(l32 == z * 8 + e32 % 4, co, 0.0), axis=1, keepdims=True)
+    co = jnp.sum(jnp.where(own_lane, co, 0.0), axis=1, keepdims=True)
     g_pos = (group_q * co).astype(BF16)
-    shift = pick(l32 == k * 32 + e32)
     g_pos = dot(g_pos, shift, (0, 0)).astype(BF16)
     for e in range(4):
         gs[e, 0:32, :] = g_part[e * 32 : e * 32 + 32, :]
         gs[e, 32:64, :] = g_pos[e * 32 : e * 32 + 32, :]
     gr[k] = gs[k]
 
-    @pl.loop(1, 4)
-    def _(i):
-        to = (k + i) % 4
-        send(gs.at[to], gr.at[k], psend.at[7], gx.at[0], quarter_peer(i))
+    for n, to in quarter:
+        send(gs.at[n], gr.at[k], psend.at[7], gx.at[0], to)
 
     leaving.append((gr.at[pl.ds(0, 3)], psend.at[7]))
 
@@ -409,40 +406,45 @@
             rss[e * 2 + t % 2 + 8 * (t // 2)] = term[(t // 2) * 16 : (t // 2) * 16 + 16, (t % 2) * 128 : (t % 2) * 128 + 128]
     rsr[z] = rss[z]
 
-    @pl.loop(0, NZ - 1)
-    def _(n):
-        to = z_at(n)
-        send(rss.at[to], rsr.at[z], psend.at[8], zr.at[0], z_peer(to))
+    for n, to in column:
+        send(rss.at[n], rsr.at[z], psend.at[8], zr.at[0], to)
 
     leaving.append((rsr.at[pl.ds(0, NZ - 1)], psend.at[8]))
 
     take_all(rsr.at[pl.ds(0, NZ - 1)], zr.at[0])
     agr[k, z] = jnp.sum(rsr[...].astype(F32), axis=0).astype(BF16)
 
-    @pl.loop(0, NZ - 1)
-    def _(n):
-        send(agr.at[k, z], agr.at[k, z], psend.at[9], za.at[0], z_peer(z_at(n)))
+    for _, to in column:
+        send(agr.at[k, z], agr.at[k, z], psend.at[9], za.at[0], to)
 
     leaving.append((agr.at[0, pl.ds(0, NZ - 1)], psend.at[9]))
 
     take_all(agr.at[k, pl.ds(0, NZ - 1)], za.at[0])
 
-    @pl.loop(1, 4)
-    def _(i):
-        send(agr.at[k], agr.at[k], psend.at[10], ga.at[0], quarter_peer(i))
+    for _, to in quarter:
+        send(agr.at[k], agr.at[k], psend.at[10], ga.at[0], to)
 
     leaving.append((agr.at[pl.ds(0, 3)], psend.at[10]))
 
     take_all(agr.at[pl.ds(0, 3)], ga.at[0])
-    for e in range(4):
-        for t in range(NZ):
-            row, at = e * 32 + (t // 8) * 16, (t % 8) * 128
-            hg[row : row + 16, at : at + 128] = agr[e, t].astype(F32)
+    grads[...] = agr[...]
 
     for copy in sent:
         copy.wait_send()
     for ref, sem in leaving:
         take_all(ref, sem)
+
+
+def finish(emb_in, loss_in, parts, emb, loss, hg):
+    z = rem(div(lax.axis_index("dp"), 2), NZ)
+    emb[...] = emb_in[...]
+    row, lane = loss_in[0:1, :], iota((1, 128), 1)
+    for i in range(4):
+        loss[i] = jnp.sum(jnp.where(lane == z * 8 + i, row, 0.0))
+    for e in range(4):
+        for t in range(NZ):
+            row, at = e * 32 + (t // 8) * 16, (t % 8) * 128
+            hg[row : row + 16, at : at + 128] = parts[e, t].astype(F32)
 
 
 def body(
@@ -450,12 +452,12 @@
 ):
     vmem = pl.BlockSpec(memory_space=pltpu.VMEM)
     V, S = pltpu.VMEM, pltpu.SemaphoreType.DMA
-    embedded, loss, head_grad = pl.pallas_call(
+    parts = pl.pallas_call(
         kernel,
         out_shape=(
             jax.ShapeDtypeStruct((4, 1024), BF16),
             jax.ShapeDtypeStruct((8, 128), F32),
-            jax.ShapeDtypeStruct((128, 1024), F32),
+            jax.ShapeDtypeStruct((4, NZ, 16, 128), BF16),
         ),
         in_specs=[pl.BlockSpec(memory_space=pl.ANY)] * 11,
         out_specs=(vmem,) * 3,
@@ -488,6 +490,7 @@
             V((128, 128), F32),
             V((4, 128, 256), BF16),
             V((4, 128, 256), BF16),
+            V((4, 128, 512), BF16),
             V((NZ, 8, 128), F32),
             V((NF, 80, 128), BF16),
             V((4, 64, 128), BF16),
@@ -496,7 +499,7 @@
             V((NZ, 16, 128), BF16),
             V((4, NZ, 16, 128), BF16),
         ]
-        + [S((S1 + S2, 7)), S((S1 + S2, 2)), S((S1 + S2, 2)), S((S1 + S2, 16)), S((2,))]
+        + [S((NS, 7)), S((NS, 2)), S((NS, 2)), S((NS, 16)), S((2,))]
         + [S((1,))] * 11
         + [S((11,))],
         compiler_params=pltpu.CompilerParams(
@@ -515,8 +518,16 @@
         positive_rows,
         neg_ids,
     )
-    z = (lax.axis_index("dp") // 2) % NZ
-    return embedded, lax.dynamic_slice_in_dim(loss[0], z * 8, 4), head_grad
+    return pl.pallas_call(
+        finish,
+        out_shape=(
+            jax.ShapeDtypeStruct((4, 1024), BF16),
+            jax.ShapeDtypeStruct((4,), F32),
+            jax.ShapeDtypeStruct((128, 1024), F32),
+        ),
+        in_specs=[vmem] * 3,
+        out_specs=(vmem, pl.BlockSpec(memory_space=pltpu.SMEM), vmem),
+    )(*parts)
 
 
 def solution(mesh):

time: 98.5 us -> 89.7 us (0.911)
  local copies, waits for them, and re-layouts: 4.45 us -> 0 us
  Pallas kernels: 93.1 us -> 88.9 us
    pallas_call x1, Pallas kernels: 93.1 us -> 87.1 us  [body(): pl.pallas_call(kernel, out_shape=(jax.ShapeDtypeStruct((4, 1024), BF16),...]
    unnamed x2 -> x0, local copies, waits for them, and re-layouts: 3.18 us -> none
    pallas_call x0 -> x1, Pallas kernels: none -> 1.81 us  [body(): pl.pallas_call(finish, out_shape=(jax.ShapeDtypeStruct((4, 1024), BF16),...]
where the time goes in v3:
time: 89.7 us; the launch traced here: 89.5 us
  Pallas kernels  88.9 us (99%)
    pallas_call x1, Pallas kernels, body(): pl.pallas_call(kernel, out_shape=(jax.ShapeDtypeStruct((4, 1024), BF16),...  87.1 us
    pallas_call x1, Pallas kernels, body(): pl.pallas_call(finish, out_shape=(jax.ShapeDtypeStruct((4, 1024), BF16),...  1.81 us

profile of v3, /device:TPU:1, one launch (start us, length us, event | category | flops | bytes accessed | tf_op | source)
XLA Modules:
  0.0 89.5 jit_solution(10278244024170621181)
XLA Ops:
  0.6 87.1 %shard_map.130 = (bf16[4,1024]{1,0:T(4,128)(2,1)}, f32[8,128]{1,0:T(8,128)}, bf16[4,16,16,128]{3,2,1,0:T(8,128)(2,1)}) custom-call(bf16[512,1024]{1,0:T(8,128)(2,1)} %tok_h.1, bf16[2,2,32,2048]{3,2,1,0:T(8,128)(2,1)} %bitcast.6, f32[1,2048]{1,0:T(1,128)} %bitcast.8, bf16[2,2,64,1024]{3,2,1,0:T(8,128)(2,1)} %bitcast.7, f32[1,1024]{1,0:T(1,128)} %bitcast.9, ...), custom_call_target="tpu_custom_call" | custom-call | tf_op jit(solution)/shard_map/pallas_call | solution.py:455
  87.7 1.8 %shard_map.131 = (bf16[4,1024]{1,0:T(4,128)(2,1)}, f32[4]{0:T(128)}, f32[128,1024]{1,0:T(8,128)}) custom-call(bf16[4,1024]{1,0:T(4,128)(2,1)} %get-tuple-element.6.emb_in, f32[8,128]{1,0:T(8,128)} %get-tuple-element.7.loss_in, bf16[4,16,16,128]{3,2,1,0:T(8,128)(2,1)} %get-tuple-element.8.parts), custom_call_target="tpu_custom_call" | custom-call | tf_op jit(solution)/shard_map/pallas_call | solution.py:521

commit v4 on v3

--- a/solution.py
+++ b/solution.py
@@ -411,6 +411,12 @@
 
     leaving.append((rsr.at[pl.ds(0, NZ - 1)], psend.at[8]))
 
+    for copy in sent:
+        copy.wait_send()
+    early = len(leaving)
+    for ref, sem in leaving:
+        take_all(ref, sem)
+
     take_all(rsr.at[pl.ds(0, NZ - 1)], zr.at[0])
     agr[k, z] = jnp.sum(rsr[...].astype(F32), axis=0).astype(BF16)
 
@@ -429,9 +435,7 @@
     take_all(agr.at[pl.ds(0, 3)], ga.at[0])
     grads[...] = agr[...]
 
-    for copy in sent:
-        copy.wait_send()
-    for ref, sem in leaving:
+    for ref, sem in leaving[early:]:
         take_all(ref, sem)
 
 

time: 89.7 us -> 89.6 us (level)
  no operation moved by 1% of the time
where the time goes in v4:
time: 89.6 us; the launch traced here: 89.4 us
  Pallas kernels  88.8 us (99%)
    pallas_call x1, Pallas kernels, body(): pl.pallas_call(kernel, out_shape=(jax.ShapeDtypeStruct((4, 1024), BF16),...  86.9 us
    pallas_call x1, Pallas kernels, body(): pl.pallas_call(finish, out_shape=(jax.ShapeDtypeStruct((4, 1024), BF16),...  1.81 us

profile of v4, /device:TPU:1, one launch (start us, length us, event | category | flops | bytes accessed | tf_op | source)
XLA Modules:
  0.0 89.4 jit_solution(10613765498838387125)
XLA Ops:
  0.6 86.9 %shard_map.130 = (bf16[4,1024]{1,0:T(4,128)(2,1)}, f32[8,128]{1,0:T(8,128)}, bf16[4,16,16,128]{3,2,1,0:T(8,128)(2,1)}) custom-call(bf16[512,1024]{1,0:T(8,128)(2,1)} %tok_h.1, bf16[2,2,32,2048]{3,2,1,0:T(8,128)(2,1)} %bitcast.6, f32[1,2048]{1,0:T(1,128)} %bitcast.8, bf16[2,2,64,1024]{3,2,1,0:T(8,128)(2,1)} %bitcast.7, f32[1,1024]{1,0:T(1,128)} %bitcast.9, ...), custom_call_target="tpu_custom_call" | custom-call | tf_op jit(solution)/shard_map/pallas_call | solution.py:459
  87.6 1.8 %shard_map.131 = (bf16[4,1024]{1,0:T(4,128)(2,1)}, f32[4]{0:T(128)}, f32[128,1024]{1,0:T(8,128)}) custom-call(bf16[4,1024]{1,0:T(4,128)(2,1)} %get-tuple-element.6.emb_in, f32[8,128]{1,0:T(8,128)} %get-tuple-element.7.loss_in, bf16[4,16,16,128]{3,2,1,0:T(8,128)(2,1)} %get-tuple-element.8.parts), custom_call_target="tpu_custom_call" | custom-call | tf_op jit(solution)/shard_map/pallas_call | solution.py:525
